TPU v7x, 512 devices: a whole 4x4x16 slice. The times are simulated.
512 devices in a mesh: dp: 16 (over z_lo, core), tensor: 4 (over y), expert: 8 (over x, z_hi).
Axes of the slice: x: 4, y: 4, z: 16 (z_hi: 2, z_lo: 8; z = z_hi * 8 + z_lo), core: 2. Of those that a mesh axis runs over, the one named last changes fastest.
Arguments:
- latent: bfloat16 [131072, 384], P(('dp', 'expert')), may hold values from -20 to 20
- out_grad: bfloat16 [131072, 64, 128], P(('dp', 'expert'), 'tensor'), may hold values from -20000 to 20000
- lengths: int32 [2, 256], P(None, ('dp', 'expert')), may hold values from 85 to 512, as said below
- momentum: float32 [128, 384, 64], P(('dp', 'expert'), None, 'tensor'), may hold values from -1.5 to 1.5
- accumulated: float32 [128, 384, 64], P(('dp', 'expert'), None, 'tensor'), may hold values from -1.5 to 1.5
Outputs:
- update: float32 [128, 384, 64], P(('dp', 'expert'), None, 'tensor')
- momentum_new: float32 [128, 384, 64], P(('dp', 'expert'), None, 'tensor')
Inputs may be any that keep to these rules, and one draw needn't show every extreme that they name: `lengths`: slots at or past a sequence's length are padding.
All inputs are finite; a program needn't handle non-finite values.
Results may differ from a plain program's by a relative error of at most 0.035.
Values may be sent and summed in bfloat16 or wider, within the bound.
A program may use at most 64 MiB of HBM per device.

v0:
```python
import math

import jax
import jax.numpy as jnp
from jax import lax
from jax.sharding import PartitionSpec as P

ITERS = 5


EPSILON = 1e-07
COEFF_A = 3.4445
COEFF_B = -4.775
COEFF_C = 2.0315
DECAY = 0.95


def orthogonalize(iterate):
    for iteration in range(ITERS):
        gram = jnp.einsum("mrc,mrd->mcd", iterate, iterate, preferred_element_type=jnp.float32)
        squared = jnp.einsum("mcd,mde->mce", gram, gram, precision=lax.Precision.HIGHEST)
        poly = (COEFF_B * gram + COEFF_C * squared).astype(jnp.bfloat16)
        moved = jnp.einsum("mrc,mce->mre", iterate, poly, preferred_element_type=jnp.float32)
        iterate = (COEFF_A * iterate.astype(jnp.float32) + moved).astype(jnp.bfloat16)
    return iterate


def per_device(latent, out_grad, lengths, momentum, accumulated):
    tok_rows = latent.shape[0]
    seq_count = lengths.shape[1]
    seq_length = tok_rows // seq_count
    limits = lengths[lengths.shape[0] - 1]
    keep_rows = (jnp.arange(seq_length, dtype=jnp.int32)[None, :] < limits[:, None]).reshape(
        tok_rows
    )
    masked = jnp.where(keep_rows[:, None], latent, jnp.zeros_like(latent))
    latent_width = latent.shape[1]
    columns = out_grad.shape[1]
    matrices = out_grad.shape[2]
    flat_grad = out_grad.reshape(tok_rows, columns * matrices)
    local_grad = lax.dot_general(
        masked, flat_grad, (((0,), (0,)), ((), ())), preferred_element_type=jnp.float32
    )
    local_grad = local_grad.reshape(latent_width, columns, matrices)
    token_total = lax.psum(jnp.sum(lengths, dtype=jnp.int32), ("dp", "expert"))
    owned_sum = lax.psum_scatter(local_grad, ("dp", "expert"), scatter_dimension=2, tiled=True)
    grad_owned = jnp.transpose(owned_sum, (2, 0, 1))
    combined = DECAY * momentum + accumulated + grad_owned / token_total.astype(jnp.float32)
    gathered = lax.all_gather(combined, "tensor", axis=2, tiled=True)
    norms = jnp.sqrt(jnp.sum(gathered * gathered, axis=(1, 2)))
    iterate = (gathered / (norms + EPSILON)[:, None, None]).astype(jnp.bfloat16)
    iterate = orthogonalize(iterate)
    full_width = iterate.shape[2]
    factor = 0.2 * math.sqrt(max(latent_width, full_width))
    own_block = lax.dynamic_slice_in_dim(iterate, lax.axis_index("tensor") * columns, columns, 2)
    update = factor * own_block.astype(jnp.float32)
    return (update, combined)


def solution(mesh):
    in_specs = (
        P(("dp", "expert"), None),
        P(("dp", "expert"), "tensor", None),
        P(None, ("dp", "expert")),
        P(("dp", "expert"), None, "tensor"),
        P(("dp", "expert"), None, "tensor"),
    )
    out_specs = (P(("dp", "expert"), None, "tensor"), P(("dp", "expert"), None, "tensor"))
    return jax.shard_map(
        per_device, mesh=mesh, in_specs=in_specs, out_specs=out_specs, check_vma=False
    )
```

profile of v0, /device:TPU:1, one launch (start us, length us, event | category | flops | bytes accessed | tf_op | source)
XLA Modules:
  0.0 1055.7 jit_solution(5360604799998685286)
XLA Ops:
  7.2 0.0 reduce-scatter.2.cloned.1.call-start
  7.2 6.3 copy.25
  13.5 0.0 copy-start.3
  13.5 0.0 copy-start.4
  13.5 6.5 copy.12
  20.0 0.0 copy-done.3
  20.0 0.1 iota_compare_fusion
  20.1 0.0 copy-done.4
  20.1 0.0 copy-start.1
  20.1 0.0 copy-start.2
  20.1 6.8 fusion
  26.9 0.0 reduce-scatter.2.cloned.1.call-update
  26.9 0.6 reduce_sum.18
  27.6 39.1 %psum.7 = s32[]{:T(128)} all-reduce(s32[]{:T(128)} %reduce_sum.18), channel_id=1, replica_groups=mesh['dp'=16,'tensor'=4,'expert'=8] {'dp','expert'}, use_global_device_ids=true, to_apply=%region_2.3 | all-reduce | flops 1 | bytes 8 | tf_op jit(solution)/shard_map/psum | solution.py:45
  67.3 966.1 %reduce-scatter.2.cloned.1.call-done = f32[384,16,1]{0,1,2:T(8,128)} async-done(((f32[384,16,128]{0,1,2:T(8,128)}), f32[384,16,1]{0,1,2:T(8,128)}) %reduce-scatter.2.cloned.1.call-update) | async-done | bytes 24592 | tf_op jit(solution)/shard_map/reduce_scatter | solution.py:46
  1033.4 0.0 copy-done.1
  1033.4 0.0 copy-done.2
  1033.4 0.7 bitcast_add_fusion
  1034.2 0.0 copy-start
  1034.2 9.9 all_gather.3
  1044.1 0.8 multiply_reduce_fusion
  1045.6 0.1 fusion.38
  1045.7 0.2 fusion.15
  1045.9 0.2 fusion.6
  1046.1 0.1 fusion.35
  1046.3 0.2 fusion.16
  1046.5 0.2 fusion.7
  1046.7 0.1 fusion.32
  1046.8 0.2 fusion.17
  1047.0 0.2 fusion.8
  1047.2 0.1 fusion.29
  1047.3 0.2 fusion.18
  1047.5 0.2 fusion.9
  1047.7 0.1 fusion.26
  1047.9 0.2 fusion.19
  1048.0 0.2 convolution_bitcast_fusion
  1048.2 0.6 convert_multiply_fusion
  1048.9 0.0 copy-done
  (4 shorter events, 0.1 us)
Async XLA Ops:
  7.2 1026.2 %reduce-scatter.2.cloned.1.call-start = ((), (), s32[]{:S(2)}) async-start(), calls=%async_computation.1 | async-start | bytes 3170304 | tf_op jit(solution)/shard_map/reduce_scatter | solution.py:46
  13.5 6.5 copy-start.3
  13.5 6.6 copy-start.4
  20.1 1013.3 %copy-start.1 = (f32[1,384,16]{1,2,0:T(8,128)S(1)}, f32[1,384,16]{1,2,0:T(8,128)}, u32[]{:S(2)}) copy-start(f32[1,384,16]{1,2,0:T(8,128)} %param.9) | copy-start | bytes 73732
  20.1 1013.3 %copy-start.2 = (f32[1,384,16]{1,2,0:T(8,128)S(1)}, f32[1,384,16]{1,2,0:T(8,128)}, u32[]{:S(2)}) copy-start(f32[1,384,16]{1,2,0:T(8,128)} %param.8) | copy-start | bytes 73732
  1034.2 14.7 %copy-start = (f32[1,384,16]{1,2,0:T(8,128)}, f32[1,384,16]{1,2,0:T(8,128)S(1)}, u32[]{:S(2)}) copy-start(f32[1,384,16]{1,2,0:T(8,128)S(1)} %bitcast_add_fusion) | copy-start | bytes 73732
Sparse Core Ops, SparseCore 0:
  27.0 1006.2 reduce-scatter.1
where the time goes:
time: 1060 us
  waiting for transfers between devices  966 us (91%)
  blocking collectives  48.9 us (5%)
  between operations  15.5 us (1%)
  local copies, waits for them, and re-layouts  12.8 us (1%)
    reduce_scatter x1, waiting for transfers between devices, per_device(): lax.psum_scatter(local_grad, ('dp', 'expert'), scatter_dimension=2, tiled...  966 us
    psum x1, blocking collectives, per_device(): token_total = lax.psum(jnp.sum(lengths, dtype=jnp.int32), ('dp', 'expert'))  39.1 us
  transfers between devices with their start and end apart: 1, of which 1 were waited for; matrix products, arithmetic and copies ran while one was open for 0% of the time, Pallas kernels for 0%

commit v1 on v0

v1 whole, which is shorter than its diff:
```python
import functools
import math

import jax
import jax.numpy as jnp
from jax import lax
from jax.experimental import pallas as pl
from jax.experimental.pallas import tpu as pltpu
from jax.sharding import PartitionSpec as P

ITERS = 5
EPSILON = 1e-07
COEFF_A = 3.4445
COEFF_B = -4.775
COEFF_C = 2.0315
DECAY = 0.95

TOK = 1024
KVR = 384
COLS = 16
MATS = 128
NX = 4
NY = 4
NZ = 16
SEQ = 512
CHUNKS = 4
NC = COLS // CHUNKS
LOADS = 4
F32 = jnp.float32
BF16 = jnp.bfloat16
MESH = pl.DeviceIdType.MESH


def device(core, x, y, z):
    return (lax.rem(z, 8) * 2 + core, y, x * 2 + z // 8)


def orthogonalize(iterate):
    for _ in range(ITERS):
        gram = lax.dot_general(
            iterate, iterate, (((1,), (1,)), ((), ())), preferred_element_type=F32
        )
        squared = jnp.dot(gram, gram, precision=lax.Precision.HIGHEST)
        poly = (COEFF_B * gram + COEFF_C * squared).astype(BF16)
        moved = jnp.dot(poly, iterate, preferred_element_type=F32)
        iterate = (COEFF_A * iterate.astype(F32) + moved).astype(BF16)
    return iterate


def kernel(
    lat_hbm, og_hbm, len_hbm, mom_hbm, acc_hbm, upd_ref, new_ref,
    lat, og, lens, mom, acc, flat, lat_t, right, turned,
    send_a, recv_a, send_x, recv_x, part, send_z, recv_z, gathered, last,
    cnt_a, cnt_x, cnt_z,
    lat_sem, og_sem, len_sem, mom_sem,
    a_ss, a_rs, x_ss, x_rs, z_ss, z_rs, y_ss, y_rs,
    ca_ss, ca_rs, cx_ss, cx_rs, cz_ss, cz_rs,
):
    dp = lax.axis_index("dp")
    y = lax.axis_index("tensor")
    expert = lax.axis_index("expert")
    core = lax.rem(dp, 2)
    x = expert // 2
    z = lax.rem(expert, 2) * 8 + dp // 2

    sibling = device(1 - core, x, y, z)
    x_peers = [device(core, lax.rem(x + d, NX), y, z) for d in range(1, NX)]
    y_peers = [device(core, x, lax.rem(y + d, NY), z) for d in range(1, NY)]
    z_order = sorted(range(1, NZ), key=lambda d: -min(d, NZ - d))
    z_peers = {d: device(core, x, y, lax.rem(z + d, NZ)) for d in z_order}

    barrier = pltpu.get_barrier_semaphore()
    for peer in [z_peers[d] for d in z_order] + x_peers + y_peers + [sibling]:
        pl.semaphore_signal(barrier, inc=1, device_id=peer, device_id_type=MESH)

    step = TOK // LOADS
    len_copy = pltpu.make_async_copy(len_hbm, lens, len_sem)
    len_copy.start()
    lat_copy = pltpu.make_async_copy(lat_hbm, lat, lat_sem)
    lat_copy.start()
    og_copies = []
    for i in range(LOADS):
        cut = pl.ds(i * step, step)
        copy = pltpu.make_async_copy(og_hbm.at[cut], og.at[cut], og_sem.at[i])
        copy.start()
        og_copies.append(copy)
    mom_copies = [
        pltpu.make_async_copy(mom_hbm, mom, mom_sem.at[0]),
        pltpu.make_async_copy(acc_hbm, acc, mom_sem.at[1]),
    ]
    for copy in mom_copies:
        copy.start()

    len_copy.wait()
    own = lens[0, 0] + lens[0, 1] + lens[1, 0] + lens[1, 1]
    cnt_a[0] = jnp.full((8, 128), own, jnp.int32)

    lat_copy.wait()
    token = lax.broadcasted_iota(jnp.int32, (TOK, 1), 0)
    limit = jnp.where(token < SEQ, lens[1, 0], lens[1, 1] + SEQ)
    masked = jnp.where(token < limit, lat[...].astype(F32), 0.0)
    lat_t[...] = masked.T.astype(BF16)

    for i in range(LOADS):
        og_copies[i].wait()

        def regroup(j, _):
            base = pl.multiple_of(i * step + j * 32, 32)
            for h in range(2):
                rows = og[pl.ds(base + h * 16, 16)].astype(F32)
                flat[h] = rows.reshape(16 * COLS, MATS)
                for c in range(COLS):
                    picked = flat[h, pl.ds(c, 16, stride=COLS), :]
                    right[c // 2, pl.ds(base + h * 16, 16), (c % 2) * MATS : (c % 2 + 1) * MATS] = (
                        picked.astype(BF16)
                    )
            return 0

        lax.fori_loop(0, step // 32, regroup, 0)

    pl.semaphore_wait(barrier, 1 + (NX - 1) + (NY - 1) + (NZ - 1))

    def count_copy(src, dst, ss, rs, peer):
        return pltpu.make_async_remote_copy(src, dst, ss, rs, device_id=peer, device_id_type=MESH)

    ca = count_copy(cnt_a.at[0], cnt_a.at[1], ca_ss, ca_rs, sibling)
    ca.start()

    def multiply(k):
        for p in range(k * NC // 2, (k + 1) * NC // 2):
            product = jnp.dot(lat_t[...], right[p], preferred_element_type=F32)
            for h in range(2):
                c = p * 2 + h
                for b in range(KVR // 128):
                    lanes = slice(b * 128, (b + 1) * 128)
                    turned[h, b] = product[lanes, h * MATS : (h + 1) * MATS].T
                    for cc in range(2):
                        for xx in range(NX):
                            q = cc * 8 + xx * 2
                            low = turned[h, b, pl.ds(q, 8, stride=16), :]
                            high = turned[h, b, pl.ds(q + 1, 8, stride=16), :]
                            send_a[k, cc, xx, c - k * NC, :, lanes] = jnp.concatenate(
                                [low, high], 0
                            ).astype(BF16)

    def core_copy(k):
        return pltpu.make_async_remote_copy(
            send_a.at[k, 1 - core], recv_a.at[k], a_ss.at[k], a_rs.at[k],
            device_id=sibling, device_id_type=MESH,
        )

    def pair_sum(k, xx):
        return send_a[k, core, xx].astype(F32) + recv_a[k, xx].astype(F32)

    def x_copy(k, d):
        return pltpu.make_async_remote_copy(
            send_x.at[k, d - 1], recv_x.at[k, d - 1], x_ss.at[k, d - 1], x_rs.at[k, d - 1],
            device_id=x_peers[d - 1], device_id_type=MESH,
        )

    def z_copy(k, d):
        return pltpu.make_async_remote_copy(
            send_z.at[k, lax.rem(z + d, NZ)], recv_z.at[k, d - 1], z_ss.at[k, d - 1], z_rs.at[k, d - 1],
            device_id=z_peers[d], device_id_type=MESH,
        )

    cx = [count_copy(cnt_x.at[0], cnt_x.at[d], cx_ss.at[d - 1], cx_rs.at[d - 1], x_peers[d - 1]) for d in range(1, NX)]
    cz = [count_copy(cnt_z.at[0], cnt_z.at[d], cz_ss.at[d - 1], cz_rs.at[d - 1], z_peers[d]) for d in range(1, NZ)]

    def start_x(k):
        core_copy(k).wait_recv()
        if k == 0:
            ca.wait_recv()
            cnt_x[0] = cnt_a[0] + cnt_a[1]
            for copy in cx:
                copy.start()
        for d in (2, 1, 3):
            send_x[k, d - 1] = pair_sum(k, lax.rem(x + d, NX)).astype(BF16)
            x_copy(k, d).start()

    def start_z(k):
        if k == 0:
            for copy in cx:
                copy.wait_recv()
            cnt_z[0] = cnt_x[0] + cnt_x[1] + cnt_x[2] + cnt_x[3]
            for copy in cz:
                copy.start()
        total = pair_sum(k, x)
        for d in (1, 3, 2):
            x_copy(k, d).wait_recv()
            total = total + recv_x[k, d - 1].astype(F32)
        total = total.reshape(NC * NZ, KVR)
        for b in range(KVR // 128):
            lanes = slice(b * 128, (b + 1) * 128)
            part[b] = total[:, lanes]
            for t in range(NZ):
                send_z[k, t, :, lanes] = part[b, pl.ds(t, NC, stride=NZ), :].astype(BF16)
        for d in z_order:
            z_copy(k, d).start()

    for k in range(CHUNKS):
        multiply(k)
        core_copy(k).start()
        if k >= 1:
            start_x(k - 1)
        if k >= 3:
            start_z(k - 3)
    start_x(CHUNKS - 1)
    for k in range(max(0, CHUNKS - 3), CHUNKS):
        start_z(k)

    for copy in mom_copies:
        copy.wait()
    count = cnt_z[0]
    for d in range(1, NZ):
        cz[d - 1].wait_recv()
        count = count + cnt_z[d]
    scale = 1.0 / count[0:1, 0:1].astype(F32)
    for k in range(CHUNKS):
        grad = send_z[k, z].astype(F32)
        for d in reversed(z_order):
            z_copy(k, d).wait_recv()
            grad = grad + recv_z[k, d - 1].astype(F32)
        cut = pl.ds(k * NC, NC)
        gathered[y, cut] = DECAY * mom[cut] + acc[cut] + grad * scale

    y_copies = [
        pltpu.make_async_remote_copy(
            gathered.at[y], gathered.at[y], y_ss.at[d - 1], y_rs.at[d - 1],
            device_id=y_peers[d - 1], device_id_type=MESH,
        )
        for d in range(1, NY)
    ]
    y_waits = [
        pltpu.make_async_remote_copy(
            gathered.at[lax.rem(y + NY - d, NY)], gathered.at[lax.rem(y + NY - d, NY)],
            y_ss.at[d - 1], y_rs.at[d - 1], device_id=y_peers[d - 1], device_id_type=MESH,
        )
        for d in range(1, NY)
    ]
    for d in (2, 1, 3):
        y_copies[d - 1].start()
    new_ref[...] = gathered[y]
    ca.wait_send()
    for k in range(CHUNKS):
        core_copy(k).wait_send()
        for d in range(1, NX):
            x_copy(k, d).wait_send()
        for d in range(1, NZ):
            z_copy(k, d).wait_send()
    for copy in cx + cz:
        copy.wait_send()
    for copy in y_waits:
        copy.wait_recv()
    full = gathered[...].reshape(NY * COLS, KVR)
    norm = jnp.sqrt(jnp.sum(full * full, axis=(0, 1), keepdims=True))
    iterate = orthogonalize((full / (norm + EPSILON)).astype(BF16))
    factor = 0.2 * math.sqrt(max(KVR, NY * COLS))
    last[...] = (factor * iterate.astype(F32)).reshape(NY, COLS, KVR)
    upd_ref[...] = last[y]
    for copy in y_copies:
        copy.wait_send()


def fused(latent, out_grad, lengths, momentum, accumulated):
    any_spec = pl.BlockSpec(memory_space=pl.ANY)
    vmem_spec = pl.BlockSpec(memory_space=pltpu.VMEM)
    block = jax.ShapeDtypeStruct((COLS, KVR), F32)
    dma = pltpu.SemaphoreType.DMA
    return pl.pallas_call(
        kernel,
        out_shape=(block, block),
        in_specs=[any_spec] * 5,
        out_specs=(vmem_spec, vmem_spec),
        scratch_shapes=[
            pltpu.VMEM((TOK, KVR), BF16),
            pltpu.VMEM((TOK, COLS, MATS), BF16),
            pltpu.SMEM((2, 2), jnp.int32),
            pltpu.VMEM((COLS, KVR), F32),
            pltpu.VMEM((COLS, KVR), F32),
            pltpu.VMEM((2, 16 * COLS, MATS), F32),
            pltpu.VMEM((KVR, TOK), BF16),
            pltpu.VMEM((COLS // 2, TOK, 2 * MATS), BF16),
            pltpu.VMEM((2, KVR // 128, MATS, 128), F32),
            pltpu.VMEM((CHUNKS, 2, NX, NC, NZ, KVR), BF16),
            pltpu.VMEM((CHUNKS, NX, NC, NZ, KVR), BF16),
            pltpu.VMEM((CHUNKS, NX - 1, NC, NZ, KVR), BF16),
            pltpu.VMEM((CHUNKS, NX - 1, NC, NZ, KVR), BF16),
            pltpu.VMEM((KVR // 128, NC * NZ, 128), F32),
            pltpu.VMEM((CHUNKS, NZ, NC, KVR), BF16),
            pltpu.VMEM((CHUNKS, NZ - 1, NC, KVR), BF16),
            pltpu.VMEM((NY, COLS, KVR), F32),
            pltpu.VMEM((NY, COLS, KVR), F32),
            pltpu.VMEM((2, 8, 128), jnp.int32),
            pltpu.VMEM((NX, 8, 128), jnp.int32),
            pltpu.VMEM((NZ, 8, 128), jnp.int32),
            dma, dma((LOADS,)), dma, dma((2,)),
            dma((CHUNKS,)), dma((CHUNKS,)),
            dma((CHUNKS, NX - 1)), dma((CHUNKS, NX - 1)),
            dma((CHUNKS, NZ - 1)), dma((CHUNKS, NZ - 1)),
            dma((NY - 1,)), dma((NY - 1,)),
            dma, dma, dma((NX - 1,)), dma((NX - 1,)), dma((NZ - 1,)), dma((NZ - 1,)),
        ],
        compiler_params=pltpu.CompilerParams(
            collective_id=0, has_side_effects=True, vmem_limit_bytes=48 << 20
        ),
        name="muon_step",
    )(latent, out_grad, lengths, momentum, accumulated)


def per_device(latent, out_grad, lengths, momentum, accumulated):
    update, combined = fused(
        latent,
        out_grad,
        lengths,
        jnp.swapaxes(momentum[0], 0, 1),
        jnp.swapaxes(accumulated[0], 0, 1),
    )
    return (jnp.swapaxes(update, 0, 1)[None], jnp.swapaxes(combined, 0, 1)[None])


def solution(mesh):
    owned = P(("dp", "expert"), None, "tensor")
    in_specs = (
        P(("dp", "expert"), None),
        P(("dp", "expert"), "tensor", None),
        P(None, ("dp", "expert")),
        owned,
        owned,
    )
    return jax.shard_map(
        per_device, mesh=mesh, in_specs=in_specs, out_specs=(owned, owned), check_vma=False
    )
```

time: 1060 us -> 52.2 us (0.05)
  waiting for transfers between devices: 966 us -> 0 us
  blocking collectives: 48.9 us -> 0 us
  Pallas kernels: 0 us -> 44 us
  between operations: 15.5 us -> 0.65 us
    reduce_scatter x1 -> x0, waiting for transfers between devices: 966 us -> none  [per_device(): lax.psum_scatter(local_grad, ('dp', 'expert'), scatter_dimension=2, tiled...]
    pallas_call x0 -> x1, Pallas kernels: none -> 44 us  [fused(): pl.pallas_call(kernel, out_shape=(block, block), in_specs=[any_spec] * 5,...]
    psum x1 -> x0, blocking collectives: 39.1 us -> none  [per_device(): token_total = lax.psum(jnp.sum(lengths, dtype=jnp.int32), ('dp', 'expert'))]
  transfers between devices with their start and end apart: 1 -> 0, of which waited for: 1 -> 0; matrix products, arithmetic and copies ran while one was open for 0% -> 0% of each run, Pallas kernels for 0% -> 0%
where the time goes in v1:
time: 52.2 us; the launch traced here: 51.3 us
  Pallas kernels  44 us (84%)
  local copies, waits for them, and re-layouts  6.68 us (13%)
  between operations  0.65 us (1%)
    pallas_call x1, Pallas kernels, fused(): pl.pallas_call(kernel, out_shape=(block, block), in_specs=[any_spec] * 5,...  44 us
    unnamed x12, local copies, waits for them, and re-layouts  6.68 us

profile of v1, /device:TPU:1, one launch (start us, length us, event | category | flops | bytes accessed | tf_op | source)
XLA Modules:
  0.0 51.3 jit_solution(4172326565458616350)
XLA Ops:
  0.6 0.0 copy-start
  0.6 2.2 %copy-done = bf16[1024,16,128]{2,1,0:T(8,128)(2,1)S(1)} copy-done((bf16[1024,16,128]{2,1,0:T(8,128)(2,1)S(1)}, bf16[1024,16,128]{2,1,0:T(8,128)(2,1)}, u32[]{:S(2)}) %copy-start) | copy-done | bytes 4194328
  2.8 0.0 copy-start.1
  2.8 1.1 %copy-done.1 = bf16[1024,384]{1,0:T(8,128)(2,1)S(1)} copy-done((bf16[1024,384]{1,0:T(8,128)(2,1)S(1)}, bf16[1024,384]{1,0:T(8,128)(2,1)}, u32[]{:S(2)}) %copy-start.1) | copy-done | bytes 786456
  4.0 0.0 copy-start.2
  4.0 0.7 %copy-done.2 = f32[1,384,16]{1,2,0:T(8,128)S(1)} copy-done((f32[1,384,16]{1,2,0:T(8,128)S(1)}, f32[1,384,16]{1,2,0:T(8,128)}, u32[]{:S(2)}) %copy-start.2) | copy-done | bytes 24600
  4.7 0.0 copy-start.3
  4.7 0.7 %copy-done.3 = f32[1,384,16]{1,2,0:T(8,128)S(1)} copy-done((f32[1,384,16]{1,2,0:T(8,128)S(1)}, f32[1,384,16]{1,2,0:T(8,128)}, u32[]{:S(2)}) %copy-start.3) | copy-done | bytes 24600
  5.4 0.0 copy-start.4
  5.4 0.7 %copy-done.4 = s32[2,2]{1,0:T(2,128)S(1)} copy-done((s32[2,2]{1,0:T(2,128)S(1)}, s32[2,2]{1,0:T(2,128)}, u32[]{:S(2)}) %copy-start.4) | copy-done | bytes 40
  6.1 44.0 %muon_step.1 = (f32[16,384]{1,0:T(8,128)S(1)}, f32[16,384]{1,0:T(8,128)S(1)}) custom-call(bf16[1024,384]{1,0:T(8,128)(2,1)S(1)} %copy-done.1, bf16[1024,16,128]{2,1,0:T(8,128)(2,1)S(1)} %copy-done, s32[2,2]{1,0:T(2,128)S(1)} %copy-done.4, f32[16,384]{1,0:T(8,128)S(1)} %bitcast.12, f32[16,384]{1,0:T(8,128)S(1)} %bitcast.13), custom_call_target="tpu_custom_call" | custom-call | tf_op jit(solution)/shard_map/muon_step/pallas_call | solution.py:270
  50.1 0.6 %copy.9 = f32[1,384,16]{1,2,0:T(8,128)} copy(f32[1,384,16]{1,2,0:T(8,128)S(1)} %bitcast.15) | data formatting | bytes 49152
  50.7 0.6 %copy.10 = f32[1,384,16]{1,2,0:T(8,128)} copy(f32[1,384,16]{1,2,0:T(8,128)S(1)} %bitcast.14) | data formatting | bytes 49152
Async XLA Ops:
  0.6 2.2 %copy-start = (bf16[1024,16,128]{2,1,0:T(8,128)(2,1)S(1)}, bf16[1024,16,128]{2,1,0:T(8,128)(2,1)}, u32[]{:S(2)}) copy-start(bf16[1024,16,128]{2,1,0:T(8,128)(2,1)} %og_hbm.1) | copy-start | bytes 12582916
  2.8 1.1 %copy-start.1 = (bf16[1024,384]{1,0:T(8,128)(2,1)S(1)}, bf16[1024,384]{1,0:T(8,128)(2,1)}, u32[]{:S(2)}) copy-start(bf16[1024,384]{1,0:T(8,128)(2,1)} %lat_hbm.1) | copy-start | bytes 2359300
  4.0 0.7 %copy-start.2 = (f32[1,384,16]{1,2,0:T(8,128)S(1)}, f32[1,384,16]{1,2,0:T(8,128)}, u32[]{:S(2)}) copy-start(f32[1,384,16]{1,2,0:T(8,128)} %param.8) | copy-start | bytes 73732
  4.7 0.7 %copy-start.3 = (f32[1,384,16]{1,2,0:T(8,128)S(1)}, f32[1,384,16]{1,2,0:T(8,128)}, u32[]{:S(2)}) copy-start(f32[1,384,16]{1,2,0:T(8,128)} %param.9) | copy-start | bytes 73732
  5.4 0.7 %copy-start.4 = (s32[2,2]{1,0:T(2,128)S(1)}, s32[2,2]{1,0:T(2,128)}, u32[]{:S(2)}) copy-start(s32[2,2]{1,0:T(2,128)} %len_hbm.1) | copy-start | bytes 52

commit v2 on v1

--- a/solution.py
+++ b/solution.py
@@ -26,6 +26,7 @@
 CHUNKS = 4
 NC = COLS // CHUNKS
 LOADS = 4
+PITCH = 17
 F32 = jnp.float32
 BF16 = jnp.bfloat16
 MESH = pl.DeviceIdType.MESH
@@ -52,7 +53,7 @@
     lat, og, lens, mom, acc, flat, lat_t, right, turned,
     send_a, recv_a, send_x, recv_x, part, send_z, recv_z, gathered, last,
     cnt_a, cnt_x, cnt_z,
-    lat_sem, og_sem, len_sem, mom_sem,
+    known, lat_sem, og_sem, len_sem, mom_sem,
     a_ss, a_rs, x_ss, x_rs, z_ss, z_rs, y_ss, y_rs,
     ca_ss, ca_rs, cx_ss, cx_rs, cz_ss, cz_rs,
 ):
@@ -70,7 +71,9 @@
     z_peers = {d: device(core, x, y, lax.rem(z + d, NZ)) for d in z_order}
 
     barrier = pltpu.get_barrier_semaphore()
-    for peer in [z_peers[d] for d in z_order] + x_peers + y_peers + [sibling]:
+    near = [x_peers[1], y_peers[1], z_peers[2], z_peers[NZ - 2], x_peers[0], x_peers[2]]
+    near += [y_peers[0], y_peers[2], z_peers[1], z_peers[NZ - 1], sibling]
+    for peer in near:
         pl.semaphore_signal(barrier, inc=1, device_id=peer, device_id_type=MESH)
 
     step = TOK // LOADS
@@ -108,23 +111,20 @@
             base = pl.multiple_of(i * step + j * 32, 32)
             for h in range(2):
                 rows = og[pl.ds(base + h * 16, 16)].astype(F32)
-                flat[h] = rows.reshape(16 * COLS, MATS)
+                for t in range(16):
+                    flat[h, pl.ds(t, COLS, stride=PITCH), :] = rows[t]
                 for c in range(COLS):
-                    picked = flat[h, pl.ds(c, 16, stride=COLS), :]
+                    picked = flat[h, pl.ds(c * PITCH, 16), :]
                     right[c // 2, pl.ds(base + h * 16, 16), (c % 2) * MATS : (c % 2 + 1) * MATS] = (
                         picked.astype(BF16)
                     )
             return 0
 
         lax.fori_loop(0, step // 32, regroup, 0)
-
-    pl.semaphore_wait(barrier, 1 + (NX - 1) + (NY - 1) + (NZ - 1))
-
-    def count_copy(src, dst, ss, rs, peer):
-        return pltpu.make_async_remote_copy(src, dst, ss, rs, device_id=peer, device_id_type=MESH)
-
-    ca = count_copy(cnt_a.at[0], cnt_a.at[1], ca_ss, ca_rs, sibling)
-    ca.start()
+        if i == LOADS // 2 - 1:
+            pl.semaphore_wait(barrier, len(near))
+            for d in (2, NZ - 2):
+                pl.semaphore_signal(known.at[0], inc=1, device_id=z_peers[d], device_id_type=MESH)
 
     def multiply(k):
         for p in range(k * NC // 2, (k + 1) * NC // 2):
@@ -133,15 +133,25 @@
                 c = p * 2 + h
                 for b in range(KVR // 128):
                     lanes = slice(b * 128, (b + 1) * 128)
-                    turned[h, b] = product[lanes, h * MATS : (h + 1) * MATS].T
+                    block = product[lanes, h * MATS : (h + 1) * MATS].T
+                    for t in range(8):
+                        turned[h, b, pl.ds(t * PITCH, 16), :] = block[t * 16 : (t + 1) * 16]
                     for cc in range(2):
                         for xx in range(NX):
                             q = cc * 8 + xx * 2
-                            low = turned[h, b, pl.ds(q, 8, stride=16), :]
-                            high = turned[h, b, pl.ds(q + 1, 8, stride=16), :]
+                            low = turned[h, b, pl.ds(q, 8, stride=PITCH), :]
+                            high = turned[h, b, pl.ds(q + 1, 8, stride=PITCH), :]
                             send_a[k, cc, xx, c - k * NC, :, lanes] = jnp.concatenate(
                                 [low, high], 0
                             ).astype(BF16)
+
+    multiply(0)
+
+    def count_copy(src, dst, ss, rs, peer):
+        return pltpu.make_async_remote_copy(src, dst, ss, rs, device_id=peer, device_id_type=MESH)
+
+    ca = count_copy(cnt_a.at[0], cnt_a.at[1], ca_ss, ca_rs, sibling)
+    ca.start()
 
     def core_copy(k):
         return pltpu.make_async_remote_copy(
@@ -189,24 +199,28 @@
         for d in (1, 3, 2):
             x_copy(k, d).wait_recv()
             total = total + recv_x[k, d - 1].astype(F32)
-        total = total.reshape(NC * NZ, KVR)
         for b in range(KVR // 128):
             lanes = slice(b * 128, (b + 1) * 128)
-            part[b] = total[:, lanes]
+            for c in range(NC):
+                part[b, pl.ds(c * PITCH, NZ), :] = total[c, :, lanes]
             for t in range(NZ):
-                send_z[k, t, :, lanes] = part[b, pl.ds(t, NC, stride=NZ), :].astype(BF16)
+                send_z[k, t, :, lanes] = part[b, pl.ds(t, NC, stride=PITCH), :].astype(BF16)
         for d in z_order:
             z_copy(k, d).start()
 
     for k in range(CHUNKS):
-        multiply(k)
+        if k >= 1:
+            multiply(k)
         core_copy(k).start()
+        if k == 1:
+            pl.semaphore_wait(known.at[0], 2)
+            for d in (4, NZ - 4):
+                pl.semaphore_signal(known.at[1], inc=1, device_id=z_peers[d], device_id_type=MESH)
         if k >= 1:
             start_x(k - 1)
-        if k >= 3:
-            start_z(k - 3)
     start_x(CHUNKS - 1)
-    for k in range(max(0, CHUNKS - 3), CHUNKS):
+    pl.semaphore_wait(known.at[1], 2)
+    for k in range(CHUNKS):
         start_z(k)
 
     for copy in mom_copies:
@@ -262,15 +276,15 @@
         copy.wait_send()
 
 
-def fused(latent, out_grad, lengths, momentum, accumulated):
-    any_spec = pl.BlockSpec(memory_space=pl.ANY)
+def fused(*operands):
+    hbm_spec = pl.BlockSpec(memory_space=pltpu.HBM)
     vmem_spec = pl.BlockSpec(memory_space=pltpu.VMEM)
     block = jax.ShapeDtypeStruct((COLS, KVR), F32)
     dma = pltpu.SemaphoreType.DMA
     return pl.pallas_call(
         kernel,
         out_shape=(block, block),
-        in_specs=[any_spec] * 5,
+        in_specs=[hbm_spec] * 5,
         out_specs=(vmem_spec, vmem_spec),
         scratch_shapes=[
             pltpu.VMEM((TOK, KVR), BF16),
@@ -278,15 +292,15 @@
             pltpu.SMEM((2, 2), jnp.int32),
             pltpu.VMEM((COLS, KVR), F32),
             pltpu.VMEM((COLS, KVR), F32),
-            pltpu.VMEM((2, 16 * COLS, MATS), F32),
+            pltpu.VMEM((2, COLS * PITCH, MATS), F32),
             pltpu.VMEM((KVR, TOK), BF16),
             pltpu.VMEM((COLS // 2, TOK, 2 * MATS), BF16),
-            pltpu.VMEM((2, KVR // 128, MATS, 128), F32),
+            pltpu.VMEM((2, KVR // 128, 8 * PITCH, 128), F32),
             pltpu.VMEM((CHUNKS, 2, NX, NC, NZ, KVR), BF16),
             pltpu.VMEM((CHUNKS, NX, NC, NZ, KVR), BF16),
             pltpu.VMEM((CHUNKS, NX - 1, NC, NZ, KVR), BF16),
             pltpu.VMEM((CHUNKS, NX - 1, NC, NZ, KVR), BF16),
-            pltpu.VMEM((KVR // 128, NC * NZ, 128), F32),
+            pltpu.VMEM((KVR // 128, NC * PITCH, 128), F32),
             pltpu.VMEM((CHUNKS, NZ, NC, KVR), BF16),
             pltpu.VMEM((CHUNKS, NZ - 1, NC, KVR), BF16),
             pltpu.VMEM((NY, COLS, KVR), F32),
@@ -294,6 +308,7 @@
             pltpu.VMEM((2, 8, 128), jnp.int32),
             pltpu.VMEM((NX, 8, 128), jnp.int32),
             pltpu.VMEM((NZ, 8, 128), jnp.int32),
+            pltpu.SemaphoreType.REGULAR((2,)),
             dma, dma((LOADS,)), dma, dma((2,)),
             dma((CHUNKS,)), dma((CHUNKS,)),
             dma((CHUNKS, NX - 1)), dma((CHUNKS, NX - 1)),
@@ -305,7 +320,7 @@
             collective_id=0, has_side_effects=True, vmem_limit_bytes=48 << 20
         ),
         name="muon_step",
-    )(latent, out_grad, lengths, momentum, accumulated)
+    )(*[pltpu.with_memory_space_constraint(v, pltpu.HBM) for v in operands])
 
 
 def per_device(latent, out_grad, lengths, momentum, accumulated):

time: 52.2 us -> 45.9 us (0.88); the launches traced: 51.3 us -> 45.6 us
  local copies, waits for them, and re-layouts: 6.68 us -> 1.22 us
    unnamed x12 -> x2, local copies, waits for them, and re-layouts: 6.68 us -> 1.22 us
where the time goes in v2:
time: 45.9 us; the launch traced here: 45.6 us
  Pallas kernels  43.7 us (95%)
  local copies, waits for them, and re-layouts  1.22 us (3%)
  between operations  0.64 us (1%)
    pallas_call x1, Pallas kernels, fused(): pl.pallas_call(kernel, out_shape=(block, block), in_specs=[hbm_spec] * 5,...  43.7 us
    unnamed x2, local copies, waits for them, and re-layouts  1.22 us

profile of v2, /device:TPU:1, one launch (start us, length us, event | category | flops | bytes accessed | tf_op | source)
XLA Modules:
  0.0 45.6 jit_solution(6339436291693038568)
XLA Ops:
  0.6 43.7 %muon_step.1 = (f32[16,384]{1,0:T(8,128)S(1)}, f32[16,384]{1,0:T(8,128)S(1)}) custom-call(bf16[1024,384]{1,0:T(8,128)(2,1)} %lat_hbm.1, bf16[1024,16,128]{2,1,0:T(8,128)(2,1)} %og_hbm.1, s32[2,2]{1,0:T(2,128)} %len_hbm.1, f32[16,384]{1,0:T(8,128)} %bitcast.14, f32[16,384]{1,0:T(8,128)} %bitcast.15), custom_call_target="tpu_custom_call" | custom-call | tf_op jit(solution)/shard_map/muon_step/pallas_call | solution.py:284
  44.4 0.6 %copy.9 = f32[1,384,16]{1,2,0:T(8,128)} copy(f32[1,384,16]{1,2,0:T(8,128)S(1)} %bitcast.13) | data formatting | bytes 49152
  45.0 0.6 %copy.10 = f32[1,384,16]{1,2,0:T(8,128)} copy(f32[1,384,16]{1,2,0:T(8,128)S(1)} %bitcast.12) | data formatting | bytes 49152

commit v3 on v2

--- a/solution.py
+++ b/solution.py
@@ -41,7 +41,13 @@
         gram = lax.dot_general(
             iterate, iterate, (((1,), (1,)), ((), ())), preferred_element_type=F32
         )
-        squared = jnp.dot(gram, gram, precision=lax.Precision.HIGHEST)
+        high = gram.astype(BF16)
+        low = (gram - high.astype(F32)).astype(BF16)
+        squared = (
+            jnp.dot(high, high, preferred_element_type=F32)
+            + jnp.dot(high, low, preferred_element_type=F32)
+            + jnp.dot(low, high, preferred_element_type=F32)
+        )
         poly = (COEFF_B * gram + COEFF_C * squared).astype(BF16)
         moved = jnp.dot(poly, iterate, preferred_element_type=F32)
         iterate = (COEFF_A * iterate.astype(F32) + moved).astype(BF16)
@@ -49,9 +55,9 @@
 
 
 def kernel(
-    lat_hbm, og_hbm, len_hbm, mom_hbm, acc_hbm, upd_ref, new_ref,
+    lat_hbm, og_hbm, len_hbm, mom_hbm, acc_hbm, all_ref,
     lat, og, lens, mom, acc, flat, lat_t, right, turned,
-    send_a, recv_a, send_x, recv_x, part, send_z, recv_z, gathered, last,
+    send_a, recv_a, send_x, recv_x, part, send_z, recv_z, gathered,
     cnt_a, cnt_x, cnt_z,
     known, lat_sem, og_sem, len_sem, mom_sem,
     a_ss, a_rs, x_ss, x_rs, z_ss, z_rs, y_ss, y_rs,
@@ -71,7 +77,8 @@
     z_peers = {d: device(core, x, y, lax.rem(z + d, NZ)) for d in z_order}
 
     barrier = pltpu.get_barrier_semaphore()
-    near = [x_peers[1], y_peers[1], z_peers[2], z_peers[NZ - 2], x_peers[0], x_peers[2]]
+    near = [z_peers[d] for d in (4, NZ - 4, 3, NZ - 3)]
+    near += [x_peers[1], y_peers[1], z_peers[2], z_peers[NZ - 2], x_peers[0], x_peers[2]]
     near += [y_peers[0], y_peers[2], z_peers[1], z_peers[NZ - 1], sibling]
     for peer in near:
         pl.semaphore_signal(barrier, inc=1, device_id=peer, device_id_type=MESH)
@@ -121,10 +128,6 @@
             return 0
 
         lax.fori_loop(0, step // 32, regroup, 0)
-        if i == LOADS // 2 - 1:
-            pl.semaphore_wait(barrier, len(near))
-            for d in (2, NZ - 2):
-                pl.semaphore_signal(known.at[0], inc=1, device_id=z_peers[d], device_id_type=MESH)
 
     def multiply(k):
         for p in range(k * NC // 2, (k + 1) * NC // 2):
@@ -146,12 +149,14 @@
                             ).astype(BF16)
 
     multiply(0)
+    pl.semaphore_wait(barrier, len(near))
+    for d in (4, NZ - 4):
+        pl.semaphore_signal(known, inc=1, device_id=z_peers[d], device_id_type=MESH)
 
     def count_copy(src, dst, ss, rs, peer):
         return pltpu.make_async_remote_copy(src, dst, ss, rs, device_id=peer, device_id_type=MESH)
 
     ca = count_copy(cnt_a.at[0], cnt_a.at[1], ca_ss, ca_rs, sibling)
-    ca.start()
 
     def core_copy(k):
         return pltpu.make_async_remote_copy(
@@ -164,128 +169,148 @@
 
     def x_copy(k, d):
         return pltpu.make_async_remote_copy(
-            send_x.at[k, d - 1], recv_x.at[k, d - 1], x_ss.at[k, d - 1], x_rs.at[k, d - 1],
+            send_x.at[k, d - 1], recv_x.at[k, d - 1], x_ss.at[k], x_rs.at[k],
             device_id=x_peers[d - 1], device_id_type=MESH,
         )
 
     def z_copy(k, d):
         return pltpu.make_async_remote_copy(
-            send_z.at[k, lax.rem(z + d, NZ)], recv_z.at[k, d - 1], z_ss.at[k, d - 1], z_rs.at[k, d - 1],
+            send_z.at[k, lax.rem(z + d, NZ)], recv_z.at[k, d - 1], z_ss.at[k], z_rs.at[k],
             device_id=z_peers[d], device_id_type=MESH,
         )
 
-    cx = [count_copy(cnt_x.at[0], cnt_x.at[d], cx_ss.at[d - 1], cx_rs.at[d - 1], x_peers[d - 1]) for d in range(1, NX)]
-    cz = [count_copy(cnt_z.at[0], cnt_z.at[d], cz_ss.at[d - 1], cz_rs.at[d - 1], z_peers[d]) for d in range(1, NZ)]
+    def settle(ref, sem):
+        pltpu.make_async_copy(ref, ref, sem).wait()
+
+    cx = [
+        count_copy(cnt_x.at[0], cnt_x.at[d], cx_ss, cx_rs, x_peers[d - 1]) for d in range(1, NX)
+    ]
+    cz = [
+        count_copy(cnt_z.at[0, 0], cnt_z.at[0, 1 + n], cz_ss.at[0], cz_rs.at[0], z_peers[d])
+        for n, d in enumerate((1, NZ - 1, 2))
+    ]
+    cw = [
+        count_copy(cnt_z.at[1, 0], cnt_z.at[1, 1 + n], cz_ss.at[1], cz_rs.at[1], z_peers[d])
+        for n, d in enumerate((4, NZ - 4, 8))
+    ]
+
+    def total_of(ref, sem):
+        settle(ref.at[pl.ds(1, 3)], sem)
+        return ref[0] + ref[1] + ref[2] + ref[3]
+
+    def start_count(k):
+        if k == 0:
+            cnt_z[0, 0] = total_of(cnt_x, cx_rs)
+            for copy in cz:
+                copy.start()
+        if k == 1:
+            cnt_z[1, 0] = total_of(cnt_z.at[0], cz_rs.at[0])
+            for copy in cw:
+                copy.start()
 
     def start_x(k):
         core_copy(k).wait_recv()
+        for d in (2, 1, 3):
+            send_x[k, d - 1] = pair_sum(k, lax.rem(x + d, NX)).astype(BF16)
+            x_copy(k, d).start()
         if k == 0:
             ca.wait_recv()
             cnt_x[0] = cnt_a[0] + cnt_a[1]
             for copy in cx:
                 copy.start()
-        for d in (2, 1, 3):
-            send_x[k, d - 1] = pair_sum(k, lax.rem(x + d, NX)).astype(BF16)
-            x_copy(k, d).start()
 
     def start_z(k):
-        if k == 0:
-            for copy in cx:
-                copy.wait_recv()
-            cnt_z[0] = cnt_x[0] + cnt_x[1] + cnt_x[2] + cnt_x[3]
-            for copy in cz:
-                copy.start()
         total = pair_sum(k, x)
+        settle(recv_x.at[k], x_rs.at[k])
         for d in (1, 3, 2):
-            x_copy(k, d).wait_recv()
             total = total + recv_x[k, d - 1].astype(F32)
         for b in range(KVR // 128):
-            lanes = slice(b * 128, (b + 1) * 128)
             for c in range(NC):
-                part[b, pl.ds(c * PITCH, NZ), :] = total[c, :, lanes]
-            for t in range(NZ):
-                send_z[k, t, :, lanes] = part[b, pl.ds(t, NC, stride=PITCH), :].astype(BF16)
-        for d in z_order:
-            z_copy(k, d).start()
+                part[b, pl.ds(c * PITCH, NZ), :] = total[c, :, b * 128 : (b + 1) * 128]
+        for d in z_order + [0]:
+            t = lax.rem(z + d, NZ)
+            for b in range(KVR // 128):
+                send_z[k, t, :, b * 128 : (b + 1) * 128] = part[b, pl.ds(t, NC, stride=PITCH), :].astype(BF16)
+            if d:
+                z_copy(k, d).start()
 
     for k in range(CHUNKS):
         if k >= 1:
             multiply(k)
         core_copy(k).start()
-        if k == 1:
-            pl.semaphore_wait(known.at[0], 2)
-            for d in (4, NZ - 4):
-                pl.semaphore_signal(known.at[1], inc=1, device_id=z_peers[d], device_id_type=MESH)
+        if k == 0:
+            ca.start()
         if k >= 1:
             start_x(k - 1)
     start_x(CHUNKS - 1)
-    pl.semaphore_wait(known.at[1], 2)
+    pl.semaphore_wait(known, 2)
     for k in range(CHUNKS):
         start_z(k)
+        start_count(k)
 
     for copy in mom_copies:
         copy.wait()
-    count = cnt_z[0]
-    for d in range(1, NZ):
-        cz[d - 1].wait_recv()
-        count = count + cnt_z[d]
+    count = total_of(cnt_z.at[1], cz_rs.at[1])
     scale = 1.0 / count[0:1, 0:1].astype(F32)
+
+    def y_copy(half, d):
+        return pltpu.make_async_remote_copy(
+            gathered.at[y, half], gathered.at[y, half], y_ss, y_rs.at[d - 1],
+            device_id=y_peers[d - 1], device_id_type=MESH,
+        )
+
     for k in range(CHUNKS):
         grad = send_z[k, z].astype(F32)
-        for d in reversed(z_order):
-            z_copy(k, d).wait_recv()
+        settle(recv_z.at[k], z_rs.at[k])
+        for d in z_order:
             grad = grad + recv_z[k, d - 1].astype(F32)
-        cut = pl.ds(k * NC, NC)
-        gathered[y, cut] = DECAY * mom[cut] + acc[cut] + grad * scale
-
-    y_copies = [
-        pltpu.make_async_remote_copy(
-            gathered.at[y], gathered.at[y], y_ss.at[d - 1], y_rs.at[d - 1],
-            device_id=y_peers[d - 1], device_id_type=MESH,
-        )
-        for d in range(1, NY)
-    ]
-    y_waits = [
-        pltpu.make_async_remote_copy(
-            gathered.at[lax.rem(y + NY - d, NY)], gathered.at[lax.rem(y + NY - d, NY)],
-            y_ss.at[d - 1], y_rs.at[d - 1], device_id=y_peers[d - 1], device_id_type=MESH,
-        )
-        for d in range(1, NY)
-    ]
-    for d in (2, 1, 3):
-        y_copies[d - 1].start()
-    new_ref[...] = gathered[y]
+        half, cut = k * NC // 8, pl.ds(k * NC % 8, NC)
+        own = pl.ds(k * NC, NC)
+        gathered[y, half, cut] = DECAY * mom[own] + acc[own] + grad * scale
+        if (k + 1) * NC % 8 == 0:
+            for d in (2, 1, 3):
+                y_copy(half, d).start()
     ca.wait_send()
     for k in range(CHUNKS):
         core_copy(k).wait_send()
-        for d in range(1, NX):
-            x_copy(k, d).wait_send()
-        for d in range(1, NZ):
-            z_copy(k, d).wait_send()
-    for copy in cx + cz:
-        copy.wait_send()
-    for copy in y_waits:
-        copy.wait_recv()
-    full = gathered[...].reshape(NY * COLS, KVR)
+        settle(recv_x.at[k], x_ss.at[k])
+        settle(recv_z.at[k], z_ss.at[k])
+    settle(cnt_x.at[pl.ds(1, NX - 1)], cx_ss)
+    for n in range(2):
+        settle(cnt_z.at[n, pl.ds(1, 3)], cz_ss.at[n])
+    for d in range(1, NY):
+        settle(gathered.at[lax.rem(y + NY - d, NY)], y_rs.at[d - 1])
+    all_ref[...] = gathered[...].reshape(NY, COLS, KVR)
+    for d in range(1, NY):
+        settle(gathered.at[y], y_ss)
+
+
+def finish(all_ref, upd_hbm, new_hbm, last, sem):
+    y = lax.axis_index("tensor")
+    keep = pltpu.make_async_copy(all_ref.at[y], new_hbm, sem.at[0])
+    keep.start()
+    full = all_ref[...].reshape(NY * COLS, KVR)
     norm = jnp.sqrt(jnp.sum(full * full, axis=(0, 1), keepdims=True))
     iterate = orthogonalize((full / (norm + EPSILON)).astype(BF16))
     factor = 0.2 * math.sqrt(max(KVR, NY * COLS))
     last[...] = (factor * iterate.astype(F32)).reshape(NY, COLS, KVR)
-    upd_ref[...] = last[y]
-    for copy in y_copies:
-        copy.wait_send()
+    out = pltpu.make_async_copy(last.at[y], upd_hbm, sem.at[1])
+    out.start()
+    keep.wait()
+    out.wait()
 
 
 def fused(*operands):
     hbm_spec = pl.BlockSpec(memory_space=pltpu.HBM)
     vmem_spec = pl.BlockSpec(memory_space=pltpu.VMEM)
+    any_spec = pl.BlockSpec(memory_space=pl.ANY)
     block = jax.ShapeDtypeStruct((COLS, KVR), F32)
     dma = pltpu.SemaphoreType.DMA
-    return pl.pallas_call(
+    gathered = pl.pallas_call(
         kernel,
-        out_shape=(block, block),
+        out_shape=jax.ShapeDtypeStruct((NY, COLS, KVR), F32),
         in_specs=[hbm_spec] * 5,
-        out_specs=(vmem_spec, vmem_spec),
+        out_specs=vmem_spec,
         scratch_shapes=[
             pltpu.VMEM((TOK, KVR), BF16),
             pltpu.VMEM((TOK, COLS, MATS), BF16),
@@ -303,24 +328,31 @@
             pltpu.VMEM((KVR // 128, NC * PITCH, 128), F32),
             pltpu.VMEM((CHUNKS, NZ, NC, KVR), BF16),
             pltpu.VMEM((CHUNKS, NZ - 1, NC, KVR), BF16),
-            pltpu.VMEM((NY, COLS, KVR), F32),
-            pltpu.VMEM((NY, COLS, KVR), F32),
+            pltpu.VMEM((NY, 2, COLS // 2, KVR), F32),
             pltpu.VMEM((2, 8, 128), jnp.int32),
             pltpu.VMEM((NX, 8, 128), jnp.int32),
-            pltpu.VMEM((NZ, 8, 128), jnp.int32),
-            pltpu.SemaphoreType.REGULAR((2,)),
+            pltpu.VMEM((2, 4, 8, 128), jnp.int32),
+            pltpu.SemaphoreType.REGULAR,
             dma, dma((LOADS,)), dma, dma((2,)),
             dma((CHUNKS,)), dma((CHUNKS,)),
-            dma((CHUNKS, NX - 1)), dma((CHUNKS, NX - 1)),
-            dma((CHUNKS, NZ - 1)), dma((CHUNKS, NZ - 1)),
-            dma((NY - 1,)), dma((NY - 1,)),
-            dma, dma, dma((NX - 1,)), dma((NX - 1,)), dma((NZ - 1,)), dma((NZ - 1,)),
+            dma((CHUNKS,)), dma((CHUNKS,)), dma((CHUNKS,)), dma((CHUNKS,)),
+            dma, dma((NY - 1,)),
+            dma, dma, dma, dma, dma((2,)), dma((2,)),
         ],
         compiler_params=pltpu.CompilerParams(
             collective_id=0, has_side_effects=True, vmem_limit_bytes=48 << 20
         ),
         name="muon_step",
     )(*[pltpu.with_memory_space_constraint(v, pltpu.HBM) for v in operands])
+    return pl.pallas_call(
+        finish,
+        out_shape=(block, block),
+        in_specs=[vmem_spec],
+        out_specs=(any_spec, any_spec),
+        scratch_shapes=[pltpu.VMEM((NY, COLS, KVR), F32), dma((2,))],
+        compiler_params=pltpu.CompilerParams(vmem_limit_bytes=8 << 20),
+        name="orthogonal_update",
+    )(gathered)
 
 
 def per_device(latent, out_grad, lengths, momentum, accumulated):

time: 45.9 us -> 43.5 us (0.948)
  local copies, waits for them, and re-layouts: 1.22 us -> 0 us
  Pallas kernels: 43.7 us -> 42.6 us
    unnamed x2 -> x0, local copies, waits for them, and re-layouts: 1.22 us -> none
    pallas_call x1 -> x2, Pallas kernels: 43.7 us -> 42.6 us  [the longest x1 39.7 us: fused(): pl.pallas_call(kernel, out_shape=jax.ShapeDtypeStruct((NY, COLS, KVR), F3...]
where the time goes in v3:
time: 43.5 us; the launch traced here: 43.2 us
  Pallas kernels  42.6 us (98%)
  between operations  0.64 us (1%)
    pallas_call x1, Pallas kernels, fused(): pl.pallas_call(kernel, out_shape=jax.ShapeDtypeStruct((NY, COLS, KVR), F3...  39.7 us
    pallas_call x1, Pallas kernels, fused(): pl.pallas_call(finish, out_shape=(block, block), in_specs=[vmem_spec], ou...  2.89 us

profile of v3, /device:TPU:1, one launch (start us, length us, event | category | flops | bytes accessed | tf_op | source)
XLA Modules:
  0.0 43.2 jit_solution(4574809009471721473)
XLA Ops:
  0.6 39.7 %muon_step.1.all_ref = f32[4,16,384]{2,1,0:T(8,128)S(1)} custom-call(bf16[1024,384]{1,0:T(8,128)(2,1)} %lat_hbm.1, bf16[1024,16,128]{2,1,0:T(8,128)(2,1)} %og_hbm.1, s32[2,2]{1,0:T(2,128)} %len_hbm.1, f32[16,384]{1,0:T(8,128)} %bitcast.12, f32[16,384]{1,0:T(8,128)} %bitcast.13), custom_call_target="tpu_custom_call" | custom-call | tf_op jit(solution)/shard_map/muon_step/pallas_call | solution.py:309
  40.3 2.9 %orthogonal_update.1 = (f32[16,384]{1,0:T(8,128)}, f32[16,384]{1,0:T(8,128)}) custom-call(f32[4,16,384]{2,1,0:T(8,128)S(1)} %muon_step.1.all_ref), custom_call_target="tpu_custom_call" | custom-call | tf_op jit(solution)/shard_map/orthogonal_update/pallas_call | solution.py:347

commit v4 on v3

--- a/solution.py
+++ b/solution.py
@@ -37,10 +37,14 @@
 
 
 def orthogonalize(iterate):
-    for _ in range(ITERS):
+    wide = iterate.astype(F32)
+    scale = 1.0 / (jnp.sqrt(jnp.sum(wide * wide, axis=(0, 1), keepdims=True)) + EPSILON)
+    for step in range(ITERS):
         gram = lax.dot_general(
             iterate, iterate, (((1,), (1,)), ((), ())), preferred_element_type=F32
         )
+        if step == 0:
+            gram = gram * scale * scale
         high = gram.astype(BF16)
         low = (gram - high.astype(F32)).astype(BF16)
         squared = (
@@ -49,13 +53,15 @@
             + jnp.dot(low, high, preferred_element_type=F32)
         )
         poly = (COEFF_B * gram + COEFF_C * squared).astype(BF16)
-        moved = jnp.dot(poly, iterate, preferred_element_type=F32)
-        iterate = (COEFF_A * iterate.astype(F32) + moved).astype(BF16)
+        moved = COEFF_A * iterate.astype(F32) + jnp.dot(poly, iterate, preferred_element_type=F32)
+        if step == 0:
+            moved = moved * scale
+        iterate = moved.astype(BF16)
     return iterate
 
 
 def kernel(
-    lat_hbm, og_hbm, len_hbm, mom_hbm, acc_hbm, all_ref,
+    lat_hbm, og_hbm, len_hbm, mom_hbm, acc_hbm, all_ref, new_ref,
     lat, og, lens, mom, acc, flat, lat_t, right, turned,
     send_a, recv_a, send_x, recv_x, part, send_z, recv_z, gathered,
     cnt_a, cnt_x, cnt_z,
@@ -76,13 +82,6 @@
     z_order = sorted(range(1, NZ), key=lambda d: -min(d, NZ - d))
     z_peers = {d: device(core, x, y, lax.rem(z + d, NZ)) for d in z_order}
 
-    barrier = pltpu.get_barrier_semaphore()
-    near = [z_peers[d] for d in (4, NZ - 4, 3, NZ - 3)]
-    near += [x_peers[1], y_peers[1], z_peers[2], z_peers[NZ - 2], x_peers[0], x_peers[2]]
-    near += [y_peers[0], y_peers[2], z_peers[1], z_peers[NZ - 1], sibling]
-    for peer in near:
-        pl.semaphore_signal(barrier, inc=1, device_id=peer, device_id_type=MESH)
-
     step = TOK // LOADS
     len_copy = pltpu.make_async_copy(len_hbm, lens, len_sem)
     len_copy.start()
@@ -94,6 +93,13 @@
         copy = pltpu.make_async_copy(og_hbm.at[cut], og.at[cut], og_sem.at[i])
         copy.start()
         og_copies.append(copy)
+    barrier = pltpu.get_barrier_semaphore()
+    near = [z_peers[d] for d in (4, NZ - 4, 3, NZ - 3)]
+    near += [x_peers[1], y_peers[1], z_peers[2], z_peers[NZ - 2], x_peers[0], x_peers[2]]
+    near += [y_peers[0], y_peers[2], z_peers[1], z_peers[NZ - 1], sibling]
+    for peer in near:
+        pl.semaphore_signal(barrier, inc=1, device_id=peer, device_id_type=MESH)
+
     mom_copies = [
         pltpu.make_async_copy(mom_hbm, mom, mom_sem.at[0]),
         pltpu.make_async_copy(acc_hbm, acc, mom_sem.at[1]),
@@ -148,10 +154,10 @@
                                 [low, high], 0
                             ).astype(BF16)
 
-    multiply(0)
     pl.semaphore_wait(barrier, len(near))
     for d in (4, NZ - 4):
         pl.semaphore_signal(known, inc=1, device_id=z_peers[d], device_id_type=MESH)
+    multiply(0)
 
     def count_copy(src, dst, ss, rs, peer):
         return pltpu.make_async_remote_copy(src, dst, ss, rs, device_id=peer, device_id_type=MESH)
@@ -253,23 +259,23 @@
     count = total_of(cnt_z.at[1], cz_rs.at[1])
     scale = 1.0 / count[0:1, 0:1].astype(F32)
 
-    def y_copy(half, d):
-        return pltpu.make_async_remote_copy(
-            gathered.at[y, half], gathered.at[y, half], y_ss, y_rs.at[d - 1],
-            device_id=y_peers[d - 1], device_id_type=MESH,
-        )
-
     for k in range(CHUNKS):
         grad = send_z[k, z].astype(F32)
         settle(recv_z.at[k], z_rs.at[k])
         for d in z_order:
             grad = grad + recv_z[k, d - 1].astype(F32)
-        half, cut = k * NC // 8, pl.ds(k * NC % 8, NC)
         own = pl.ds(k * NC, NC)
-        gathered[y, half, cut] = DECAY * mom[own] + acc[own] + grad * scale
-        if (k + 1) * NC % 8 == 0:
-            for d in (2, 1, 3):
-                y_copy(half, d).start()
+        new_ref[own] = DECAY * mom[own] + acc[own] + grad * scale
+    gathered[y] = new_ref[...].astype(BF16)
+
+    def y_copy(d):
+        return pltpu.make_async_remote_copy(
+            gathered.at[y], gathered.at[y], y_ss, y_rs.at[d - 1],
+            device_id=y_peers[d - 1], device_id_type=MESH,
+        )
+
+    for d in (2, 1, 3):
+        y_copy(d).start()
     ca.wait_send()
     for k in range(CHUNKS):
         core_copy(k).wait_send()
@@ -280,18 +286,16 @@
         settle(cnt_z.at[n, pl.ds(1, 3)], cz_ss.at[n])
     for d in range(1, NY):
         settle(gathered.at[lax.rem(y + NY - d, NY)], y_rs.at[d - 1])
-    all_ref[...] = gathered[...].reshape(NY, COLS, KVR)
+    all_ref[...] = gathered[...]
     for d in range(1, NY):
-        settle(gathered.at[y], y_ss)
-
-
-def finish(all_ref, upd_hbm, new_hbm, last, sem):
+        y_copy(d).wait_send()
+
+
+def finish(all_ref, own_ref, upd_hbm, new_hbm, last, sem):
     y = lax.axis_index("tensor")
-    keep = pltpu.make_async_copy(all_ref.at[y], new_hbm, sem.at[0])
+    keep = pltpu.make_async_copy(own_ref, new_hbm, sem.at[0])
     keep.start()
-    full = all_ref[...].reshape(NY * COLS, KVR)
-    norm = jnp.sqrt(jnp.sum(full * full, axis=(0, 1), keepdims=True))
-    iterate = orthogonalize((full / (norm + EPSILON)).astype(BF16))
+    iterate = orthogonalize(all_ref[...].reshape(NY * COLS, KVR))
     factor = 0.2 * math.sqrt(max(KVR, NY * COLS))
     last[...] = (factor * iterate.astype(F32)).reshape(NY, COLS, KVR)
     out = pltpu.make_async_copy(last.at[y], upd_hbm, sem.at[1])
@@ -306,11 +310,11 @@
     any_spec = pl.BlockSpec(memory_space=pl.ANY)
     block = jax.ShapeDtypeStruct((COLS, KVR), F32)
     dma = pltpu.SemaphoreType.DMA
-    gathered = pl.pallas_call(
+    gathered, combined = pl.pallas_call(
         kernel,
-        out_shape=jax.ShapeDtypeStruct((NY, COLS, KVR), F32),
+        out_shape=(jax.ShapeDtypeStruct((NY, COLS, KVR), BF16), block),
         in_specs=[hbm_spec] * 5,
-        out_specs=vmem_spec,
+        out_specs=(vmem_spec, vmem_spec),
         scratch_shapes=[
             pltpu.VMEM((TOK, KVR), BF16),
             pltpu.VMEM((TOK, COLS, MATS), BF16),
@@ -328,7 +332,7 @@
             pltpu.VMEM((KVR // 128, NC * PITCH, 128), F32),
             pltpu.VMEM((CHUNKS, NZ, NC, KVR), BF16),
             pltpu.VMEM((CHUNKS, NZ - 1, NC, KVR), BF16),
-            pltpu.VMEM((NY, 2, COLS // 2, KVR), F32),
+            pltpu.VMEM((NY, COLS, KVR), BF16),
             pltpu.VMEM((2, 8, 128), jnp.int32),
             pltpu.VMEM((NX, 8, 128), jnp.int32),
             pltpu.VMEM((2, 4, 8, 128), jnp.int32),
@@ -347,12 +351,12 @@
     return pl.pallas_call(
         finish,
         out_shape=(block, block),
-        in_specs=[vmem_spec],
+        in_specs=[vmem_spec, vmem_spec],
         out_specs=(any_spec, any_spec),
         scratch_shapes=[pltpu.VMEM((NY, COLS, KVR), F32), dma((2,))],
         compiler_params=pltpu.CompilerParams(vmem_limit_bytes=8 << 20),
         name="orthogonal_update",
-    )(gathered)
+    )(gathered, combined)
 
 
 def per_device(latent, out_grad, lengths, momentum, accumulated):

time: 43.5 us -> 43 us (0.989)
  Pallas kernels: 42.6 us -> 41.8 us
    pallas_call x2, Pallas kernels: 42.6 us -> 41.8 us  [the longest x1 39.1 us: fused(): pl.pallas_call(kernel, out_shape=(jax.ShapeDtypeStruct((NY, COLS, KVR), B...]
where the time goes in v4:
time: 43 us; the launch traced here: 42.5 us
  Pallas kernels  41.8 us (97%)
  between operations  0.64 us (1%)
    pallas_call x1, Pallas kernels, fused(): pl.pallas_call(kernel, out_shape=(jax.ShapeDtypeStruct((NY, COLS, KVR), B...  39.1 us
    pallas_call x1, Pallas kernels, fused(): pl.pallas_call(finish, out_shape=(block, block), in_specs=[vmem_spec, vme...  2.75 us

profile of v4, /device:TPU:1, one launch (start us, length us, event | category | flops | bytes accessed | tf_op | source)
XLA Modules:
  0.0 42.5 jit_solution(1544055251698448769)
XLA Ops:
  0.6 39.1 %muon_step.1 = (bf16[4,16,384]{2,1,0:T(8,128)(2,1)S(1)}, f32[16,384]{1,0:T(8,128)S(1)}) custom-call(bf16[1024,384]{1,0:T(8,128)(2,1)} %lat_hbm.1, bf16[1024,16,128]{2,1,0:T(8,128)(2,1)} %og_hbm.1, s32[2,2]{1,0:T(2,128)} %len_hbm.1, f32[16,384]{1,0:T(8,128)} %bitcast.12, f32[16,384]{1,0:T(8,128)} %bitcast.13), custom_call_target="tpu_custom_call" | custom-call | tf_op jit(solution)/shard_map/muon_step/pallas_call | solution.py:313
  39.7 2.8 %orthogonal_update.1 = (f32[16,384]{1,0:T(8,128)}, f32[16,384]{1,0:T(8,128)}) custom-call(bf16[4,16,384]{2,1,0:T(8,128)(2,1)S(1)} %get-tuple-element.6.all_ref, f32[16,384]{1,0:T(8,128)S(1)} %get-tuple-element.7.own_ref), custom_call_target="tpu_custom_call" | custom-call | tf_op jit(solution)/shard_map/orthogonal_update/pallas_call | solution.py:351

commit v5 on v4

--- a/solution.py
+++ b/solution.py
@@ -25,7 +25,7 @@
 SEQ = 512
 CHUNKS = 4
 NC = COLS // CHUNKS
-LOADS = 4
+LOADS = 2
 PITCH = 17
 F32 = jnp.float32
 BF16 = jnp.bfloat16

time: 43 us -> 42.8 us (level)
  no operation moved by 1% of the time
where the time goes in v5:
time: 42.8 us; the launch traced here: 42.3 us
  Pallas kernels  41.7 us (97%)
  between operations  0.64 us (1%)
    pallas_call x1, Pallas kernels, fused(): pl.pallas_call(kernel, out_shape=(jax.ShapeDtypeStruct((NY, COLS, KVR), B...  38.9 us
    pallas_call x1, Pallas kernels, fused(): pl.pallas_call(finish, out_shape=(block, block), in_specs=[vmem_spec, vme...  2.76 us

profile of v5, /device:TPU:1, one launch (start us, length us, event | category | flops | bytes accessed | tf_op | source)
XLA Modules:
  0.0 42.3 jit_solution(8113414886589774817)
XLA Ops:
  0.6 38.9 %muon_step.1 = (bf16[4,16,384]{2,1,0:T(8,128)(2,1)S(1)}, f32[16,384]{1,0:T(8,128)S(1)}) custom-call(bf16[1024,384]{1,0:T(8,128)(2,1)} %lat_hbm.1, bf16[1024,16,128]{2,1,0:T(8,128)(2,1)} %og_hbm.1, s32[2,2]{1,0:T(2,128)} %len_hbm.1, f32[16,384]{1,0:T(8,128)} %bitcast.12, f32[16,384]{1,0:T(8,128)} %bitcast.13), custom_call_target="tpu_custom_call" | custom-call | tf_op jit(solution)/shard_map/muon_step/pallas_call | solution.py:313
  39.6 2.8 %orthogonal_update.1 = (f32[16,384]{1,0:T(8,128)}, f32[16,384]{1,0:T(8,128)}) custom-call(bf16[4,16,384]{2,1,0:T(8,128)(2,1)S(1)} %get-tuple-element.6.all_ref, f32[16,384]{1,0:T(8,128)S(1)} %get-tuple-element.7.own_ref), custom_call_target="tpu_custom_call" | custom-call | tf_op jit(solution)/shard_map/orthogonal_update/pallas_call | solution.py:351

commit v6 on v5

--- a/solution.py
+++ b/solution.py
@@ -25,7 +25,7 @@
 SEQ = 512
 CHUNKS = 4
 NC = COLS // CHUNKS
-LOADS = 2
+LOADS = 1
 PITCH = 17
 F32 = jnp.float32
 BF16 = jnp.bfloat16

time: 42.8 us -> 43.1 us (level)
  no operation moved by 1% of the time
where the time goes in v6:
time: 43.1 us; the launch traced here: 42.7 us
  Pallas kernels  42.1 us (98%)
  between operations  0.64 us (1%)
    pallas_call x1, Pallas kernels, fused(): pl.pallas_call(kernel, out_shape=(jax.ShapeDtypeStruct((NY, COLS, KVR), B...  39.3 us
    pallas_call x1, Pallas kernels, fused(): pl.pallas_call(finish, out_shape=(block, block), in_specs=[vmem_spec, vme...  2.76 us

profile of v6, /device:TPU:1, one launch (start us, length us, event | category | flops | bytes accessed | tf_op | source)
XLA Modules:
  0.0 42.7 jit_solution(9303482930447767163)
XLA Ops:
  0.6 39.3 %muon_step.1 = (bf16[4,16,384]{2,1,0:T(8,128)(2,1)S(1)}, f32[16,384]{1,0:T(8,128)S(1)}) custom-call(bf16[1024,384]{1,0:T(8,128)(2,1)} %lat_hbm.1, bf16[1024,16,128]{2,1,0:T(8,128)(2,1)} %og_hbm.1, s32[2,2]{1,0:T(2,128)} %len_hbm.1, f32[16,384]{1,0:T(8,128)} %bitcast.12, f32[16,384]{1,0:T(8,128)} %bitcast.13), custom_call_target="tpu_custom_call" | custom-call | tf_op jit(solution)/shard_map/muon_step/pallas_call | solution.py:313
  40.0 2.8 %orthogonal_update.1 = (f32[16,384]{1,0:T(8,128)}, f32[16,384]{1,0:T(8,128)}) custom-call(bf16[4,16,384]{2,1,0:T(8,128)(2,1)S(1)} %get-tuple-element.6.all_ref, f32[16,384]{1,0:T(8,128)S(1)} %get-tuple-element.7.own_ref), custom_call_target="tpu_custom_call" | custom-call | tf_op jit(solution)/shard_map/orthogonal_update/pallas_call | solution.py:351
